TPU v7x, 32 devices: a whole 2x2x4 slice. The times are simulated.
32 devices in a mesh: lat: 4 (over x, core), lon: 8 (over z, y).
Axes of the slice: x: 2, y: 2, z: 4, core: 2. Of those that a mesh axis runs over, the one named last changes fastest.
Arguments:
- inputs_below: bfloat16 [64, 32, 1024], P(None, 'lat', 'lon'), may hold values from -6 to 6
- hidden_prev: bfloat16 [64, 32, 1024], P(None, 'lat', 'lon'), may hold values from -0.8984375 to 0.8984375
- cell_prev: float32 [64, 32, 1024], P(None, 'lat', 'lon'), may hold values from -5 to 5
- kernel_weights: bfloat16 [9, 256, 128], replicated, may hold values from -0.1875 to 0.1875
- gate_bias: float32 [256], replicated, may hold values from -4 to 4
- readout: float32 [64], replicated, may hold values from -0.75 to 0.75
- target_field: float32 [32, 1024], P('lat', 'lon'), may hold values from -6 to 6
- land_mask: int32 [32, 1024], P('lat', 'lon'), may hold values 0 or 1
- fire_mask: int32 [32, 1024], P('lat', 'lon'), may hold values 0 or 1
- hidden_grad: bfloat16 [64, 32, 1024], P(None, 'lat', 'lon'), may hold values from -10 to 10
Outputs:
- hidden_next: bfloat16 [64, 32, 1024], P(None, 'lat', 'lon')
- cell_next: float32 [64, 32, 1024], P(None, 'lat', 'lon')
- grad_inputs: bfloat16 [64, 32, 1024], P(None, 'lat', 'lon')
- grad_hidden: bfloat16 [64, 32, 1024], P(None, 'lat', 'lon')
- grad_cell: float32 [64, 32, 1024], P(None, 'lat', 'lon')
- grad_kernel: float32 [9, 256, 128], replicated
- grad_bias: float32 [256], replicated
Inputs may be any that keep to these rules, and one draw needn't show every extreme that they name: `land_mask`: 1 marks land cells, 0 sea cells. `fire_mask`: 1 marks cells where fire danger is observed.
All inputs are finite; a program needn't handle non-finite values. No bound on the sum of `land_mask` or of `fire_mask` on one device may be relied on, other than what follows from the above.
Results may differ from a plain program's by a relative error of at most 0.0049.
Values may be sent and summed in bfloat16 or wider, within the bound.
No kernel may reach another device: no remote copies, remote signals or barrier semaphores. Data moves between devices by JAX's collectives and lax.ppermute only.
A program may use at most 64 MiB of HBM per device.

v0:
```python
import functools
import math

import jax
import jax.numpy as jnp
from jax import lax
from jax.experimental import pallas as pl
from jax.experimental.pallas import tpu as pltpu
from jax.sharding import Mesh, PartitionSpec as P

F32 = jnp.float32
BF16 = jnp.bfloat16
AXES = ("band", "core", "lon")
BIAS_ROWS = 16
LAST = 16
VMEM = pl.BlockSpec(memory_space=pltpu.VMEM)
HBM = pl.BlockSpec(memory_space=pltpu.HBM)
ACROSS = (((1,), (1,)), ((), ()))


def sds(shape, dtype):
    return jax.ShapeDtypeStruct(shape, dtype)


def call(kernel, out_shape, scratch=(), remote=0, flops=0, moved=0, transcendentals=0):
    def run(*args):
        near = len(args) - remote
        far = [pltpu.with_memory_space_constraint(arg, pltpu.HBM) for arg in args[near:]]
        return pl.pallas_call(
            kernel,
            out_shape=out_shape,
            in_specs=[VMEM] * near + [HBM] * remote,
            out_specs=jax.tree.map(lambda _: VMEM, out_shape),
            scratch_shapes=list(scratch),
            cost_estimate=pl.CostEstimate(
                flops=flops, bytes_accessed=moved, transcendentals=transcendentals
            ),
            compiler_params=pltpu.CompilerParams(vmem_limit_bytes=24 * 1024 * 1024),
        )(*args[:near], *far)

    return run


class Layout:
    def __init__(self, lat_count, lon_count, kernel_rows):
        self.lat, self.lon = lat_count, lon_count
        self.half = lon_count // 2
        devices = lat_count * lon_count
        self.rows = -(-kernel_rows // (devices * 8)) * devices * 8
        self.bits = [("lat", 1 << k) for k in range(lat_count.bit_length() - 1)]
        self.bits += [("lon", 1 << k) for k in range(lon_count.bit_length() - 1)]

    def position(self):
        return 2 * lax.axis_index("band") + lax.axis_index("core"), lax.axis_index("lon")

    def rank(self, phase):
        axis, bit = self.bits[phase]
        lat, lon = self.position()
        return ((lat if axis == "lat" else lon) // bit) % 2

    def pairs(self, partner):
        result = []
        for lat in range(self.lat):
            for lon in range(self.lon):
                there = partner(lat, lon)
                result.append((lat * self.lon + lon, there[0] * self.lon + there[1]))
        return result

    def phase_pairs(self, phase):
        axis, bit = self.bits[phase]
        if axis == "lat":
            return self.pairs(lambda lat, lon: (lat ^ bit, lon))
        return self.pairs(lambda lat, lon: (lat, lon ^ bit))

    def inner_rows(self, lat, lon):
        return lat ^ 1, lon

    def outer_rows(self, lat, lon):
        there = lat + 1 if lat % 2 else lat - 1
        if 0 <= there < self.lat:
            return there, lon
        return lat, (lon + self.half) % self.lon

    def inner_columns(self, lat, lon):
        return lat, lon ^ 1

    def outer_columns(self, lat, lon):
        return lat, (lon + (1 if lon % 2 else -1)) % self.lon


def permuted(value, pairs):
    return lax.ppermute(value, AXES, pairs)


def lanes(shape):
    return lax.broadcasted_iota(jnp.int32, shape, len(shape) - 1)


def rolled(value, shift):
    shift %= value.shape[1]
    return pltpu.roll(value, shift, 1) if shift else value


def edge_columns(row, position, columns):
    lane = lanes(row.shape)
    columns = jnp.where(lane == position, rolled(row, position), columns)
    return jnp.where(lane == LAST + position, rolled(row, LAST + position + 1), columns)


def pick(flag, yes, no):
    return jnp.where(flag, yes, no)


def is_odd(axis):
    return lax.axis_index(axis) % 2 == 1


def row_sends(first, last, inner_out, outer_out):
    odd = is_odd("core")
    inner_out[...] = pick(odd, first, last).astype(BF16)
    outer_out[...] = pick(odd, last, first).astype(BF16)


def row_halo(inner, outer):
    odd = is_odd("core")
    inner, outer = inner[...].astype(F32), outer[...].astype(F32)
    return pick(odd, inner, outer), pick(odd, outer, inner)


def column_halo(inner, outer):
    odd = is_odd("lon")
    inner, outer = inner[...].astype(F32), outer[...].astype(F32)
    return pick(odd, inner, outer), pick(odd, outer, inner)


def widened(row_count, rows, row_blocks, column_blocks, emit):
    north, south = row_halo(*row_blocks)
    west, east = column_halo(*column_blocks)
    width = west.shape[1]
    lane = lanes(west.shape)
    for position in range(row_count + 2):
        if position == 0:
            row = north
        elif position == row_count + 1:
            row = south
        else:
            row = rows(position - 1)
        left = rolled(west, -LAST - position)
        right = rolled(east, width - 1 - position)
        emit(
            position,
            jnp.where(lane == 0, left, rolled(row, 1)),
            row,
            jnp.where(lane == width - 1, right, rolled(row, -1)),
        )


def pack_kernel(below, hidden, inner_out, outer_out, wide_out, below_here, hidden_here, arrived):
    first = pltpu.make_async_copy(below, below_here, arrived.at[0])
    second = pltpu.make_async_copy(hidden, hidden_here, arrived.at[1])
    first.start()
    second.start()
    channels, row_count, width = below.shape
    size = channels * row_count
    first.wait()
    wide_out[0:size, :] = below_here[...].astype(F32).reshape(size, width)
    second.wait()
    wide_out[size : 2 * size, :] = hidden_here[...].astype(F32).reshape(size, width)
    edges = [
        wide_out[pl.ds(index, 2 * channels, stride=row_count), :] for index in (0, row_count - 1)
    ]
    row_sends(edges[0], edges[1], inner_out, outer_out)


def down_rows(values, width):
    count = values.shape[0]
    return jnp.broadcast_to(values[None, :], (width, count)).T


def prepare_kernel(
    wide,
    cell_hbm,
    weights_hbm,
    hidden_grad_hbm,
    target_hbm,
    land_hbm,
    fire_hbm,
    gate_bias_hbm,
    readout_hbm,
    rows_out,
    columns_out,
    cell_out,
    weights_out,
    hidden_grad_out,
    target_out,
    land_out,
    fire_out,
    bias_wide_out,
    readout_wide_out,
    hidden_grad_here,
    gate_bias_here,
    readout_here,
    arrived,
):
    copies = [
        pltpu.make_async_copy(source, target, arrived.at[index])
        for index, (source, target) in enumerate(
            (
                (cell_hbm, cell_out),
                (weights_hbm, weights_out),
                (hidden_grad_hbm, hidden_grad_here),
                (target_hbm, target_out),
                (land_hbm, land_out),
                (fire_hbm, fire_out),
                (gate_bias_hbm, gate_bias_here),
                (readout_hbm, readout_here),
            )
        )
    ]
    for copy in copies:
        copy.start()
    row_count, channels, width = rows_out.shape
    columns = jnp.zeros((channels, width), F32)
    for index in range(row_count):
        row = wide[pl.ds(index, channels, stride=row_count), :]
        rows_out[index] = row.astype(BF16)
        columns = edge_columns(row, index + 1, columns)
    columns_out[...] = columns
    for copy in copies:
        copy.wait()
    hidden_grad_out[...] = hidden_grad_here[...].astype(F32).reshape(hidden_grad_out.shape)
    bias_wide_out[...] = down_rows(gate_bias_here[...], width)
    readout_wide_out[...] = down_rows(readout_here[...], width)


def columns_kernel(row_count, columns, inner, outer, out):
    north, south = row_halo(inner, outer)
    value = edge_columns(north, 0, columns[...].astype(F32))
    out[...] = edge_columns(south, row_count + 1, value).astype(BF16)


def encode(bias):
    high = bias.astype(BF16).astype(F32)
    return jnp.concatenate([high, bias - high], axis=0)


def decode(block):
    return block[0:8] + block[8:16]


def split_sum(place, phase, bias, sums, rows, send_out, keep_out):
    half = rows // 2
    rank = place.rank(phase)
    send_out[0:BIAS_ROWS, :] = encode(bias).astype(BF16)
    away = pl.ds(pl.multiple_of((1 - rank) * half, 8), half)
    send_out[BIAS_ROWS:, :] = sums[away, :].astype(BF16)
    keep_out[...] = sums[pl.ds(pl.multiple_of(rank * half, 8), half), :]


def gates_kernel(
    place,
    rows_in,
    inner_row,
    outer_row,
    inner_column,
    outer_column,
    cell_prev,
    weights,
    hidden_grad,
    target,
    land,
    fire,
    bias_wide,
    readout_wide,
    hidden_out,
    cell_out,
    grad_cell_out,
    pre_out,
    inner_out,
    outer_out,
    columns_out,
    send_out,
    keep_out,
    bias_out,
    shifted,
    hidden_wide,
    sums,
):
    row_count, channels, width = rows_in.shape
    gate_count = weights.shape[1]
    hid = gate_count // 4

    def emit(position, left, row, right):
        at = pl.ds(position * width, width)
        shifted[0:channels, at] = left.astype(BF16)
        shifted[channels : 2 * channels, at] = row.astype(BF16)
        shifted[2 * channels : 3 * channels, at] = right.astype(BF16)

    widened(
        row_count,
        lambda index: rows_in[index].astype(F32),
        (inner_row, outer_row),
        (inner_column, outer_column),
        emit,
    )

    taps = [
        jnp.concatenate([weights[3 * a], weights[3 * a + 1], weights[3 * a + 2]], axis=1)
        for a in range(3)
    ]
    bias_total = jnp.zeros((gate_count, width), F32)
    columns = jnp.zeros((gate_count, width), F32)
    edges = []
    readout = readout_wide[...]
    pair = 2 if row_count % 2 == 0 else 1
    for base in range(0, row_count, pair):
        preact = jnp.zeros((gate_count, pair * width), F32)
        for a in range(3):
            preact += jnp.dot(
                taps[a],
                shifted[:, pl.ds((base + a) * width, pair * width)],
                preferred_element_type=F32,
            )
        for offset in range(pair):
            index = base + offset
            strided = pl.ds(index, hid, stride=row_count)
            part = preact[:, offset * width : (offset + 1) * width] + bias_wide[...]
            input_gate = 0.5 + 0.5 * jnp.tanh(0.5 * part[0:hid])
            forget_gate = 0.5 + 0.5 * jnp.tanh(0.5 * part[hid : 2 * hid])
            output_gate = 0.5 + 0.5 * jnp.tanh(0.5 * part[2 * hid : 3 * hid])
            candidate = jnp.tanh(part[3 * hid : 4 * hid])
            cell_before = cell_prev[strided, :]
            land_row = land[index : index + 1, :].astype(F32)
            fire_row = fire[index : index + 1, :].astype(F32)
            cell_next = land_row * (forget_gate * cell_before + input_gate * candidate)
            squashed = jnp.tanh(cell_next)
            hidden_next = (output_gate * squashed).astype(BF16).astype(F32)
            predicted = jnp.sum(readout * hidden_next, axis=0, keepdims=True)
            miss = 2.0 * (fire_row * (predicted - target[index : index + 1, :]))
            total_grad = hidden_grad[strided, :] + miss * readout
            cell_grad = land_row * total_grad * output_gate * (1.0 - squashed * squashed)
            cell_out[strided, :] = cell_next
            hidden_wide[strided, :] = hidden_next
            grad_cell_out[strided, :] = cell_grad * forget_gate
            pre_grad = jnp.concatenate(
                [
                    cell_grad * candidate * input_gate * (1.0 - input_gate),
                    cell_grad * cell_before * forget_gate * (1.0 - forget_gate),
                    total_grad * squashed * output_gate * (1.0 - output_gate),
                    cell_grad * input_gate * (1.0 - candidate * candidate),
                ],
                axis=0,
            )
            bias_total += pre_grad
            columns = edge_columns(pre_grad, index + 1, columns)
            pre_out[:, pl.ds(index * width, width)] = pre_grad.astype(BF16)
            if index in (0, row_count - 1):
                edges.append(pre_grad)
    hidden_out[...] = hidden_wide[...].reshape(hidden_out.shape).astype(BF16)
    row_sends(edges[0], edges[-1], inner_out, outer_out)
    columns_out[...] = columns.astype(BF16)

    for a in range(3):
        product = lax.dot_general(
            pre_out[...],
            shifted[:, pl.ds(a * width, row_count * width)],
            ACROSS,
            preferred_element_type=F32,
        )
        for b in range(3):
            at = (3 * a + b) * gate_count
            sums[at : at + gate_count, :] = product[:, b * channels : (b + 1) * channels]
    used = 9 * gate_count
    if place.rows > used:
        sums[used:, :] = jnp.zeros((place.rows - used, channels), F32)

    ones = jnp.ones((8, width), BF16)
    high = bias_total.astype(BF16)
    low = (bias_total - high.astype(F32)).astype(BF16)
    flat = lax.dot_general(ones, high, ACROSS, preferred_element_type=F32)
    flat += lax.dot_general(ones, low, ACROSS, preferred_element_type=F32)
    odd = lax.broadcasted_iota(jnp.int32, (8, channels), 0) % 2 == 1
    bias_rows = jnp.where(odd, flat[:, channels : 2 * channels], flat[:, 0:channels])
    bias_out[...] = bias_rows
    split_sum(place, 0, bias_rows, sums, place.rows, send_out, keep_out)


def halve_kernel(place, phase, scaling, keep, bias, received, after, *outs):
    del after
    total = keep[...] + received[BIAS_ROWS:, :].astype(F32)
    bias_total = bias[...] + decode(received[0:BIAS_ROWS, :].astype(F32))
    if phase == len(place.bits) - 1:
        (out,) = outs
        out[0:BIAS_ROWS, :] = encode(bias_total * scaling).astype(BF16)
        out[BIAS_ROWS:, :] = (total * scaling).astype(BF16)
        return
    send_out, keep_out, bias_out, scratch = outs
    scratch[...] = total
    bias_out[...] = bias_total
    split_sum(place, phase + 1, bias_total, scratch, total.shape[0], send_out, keep_out)


def double_kernel(place, phase, own, received, out):
    odd = place.rank(phase) == 1
    here, there = own[...].astype(F32), received[...].astype(F32)
    first, second = pick(odd, there, here), pick(odd, here, there)
    out[...] = jnp.concatenate([first, second[BIAS_ROWS:]], axis=0).astype(BF16)


def finish_kernel(place, own, received, out, bias_out):
    odd = place.rank(0) == 1
    rows = own.shape[0] - BIAS_ROWS
    here, there = own[...].astype(F32), received[...].astype(F32)
    rank = place.rank(0)
    out[pl.ds(pl.multiple_of(rank * rows, 8), rows), :] = here[BIAS_ROWS:]
    out[pl.ds(pl.multiple_of((1 - rank) * rows, 8), rows), :] = there[BIAS_ROWS:]
    bias_out[...] = decode(pick(odd, there[0:BIAS_ROWS], here[0:BIAS_ROWS]))


def field_kernel(
    place,
    pre,
    inner_row,
    outer_row,
    inner_column,
    outer_column,
    weights,
    inputs_out,
    hidden_out,
    done_out,
    shifted,
    turned,
    wide,
):
    gate_count = pre.shape[0]
    channels = weights.shape[2]
    done_out[...] = jnp.zeros(done_out.shape, F32)
    hid, row_count, width = hidden_out.shape

    def emit(position, left, row, right):
        at = pl.ds(position * width, width)
        shifted[0:gate_count, at] = right.astype(BF16)
        shifted[gate_count : 2 * gate_count, at] = row.astype(BF16)
        shifted[2 * gate_count : 3 * gate_count, at] = left.astype(BF16)

    widened(
        row_count,
        lambda index: pre[:, pl.ds(index * width, width)].astype(F32),
        (inner_row, outer_row),
        (inner_column, outer_column),
        emit,
    )
    for a in range(3):
        for b in range(3):
            turned[a, :, b * gate_count : (b + 1) * gate_count] = weights[3 * a + b].T
    lat = place.position()[0]
    top = turned[jnp.where(lat == 0, 0, 2)]
    bottom = turned[jnp.where(lat == place.lat - 1, 2, 0)]

    def product(matrix, position, count):
        return jnp.dot(
            matrix, shifted[:, pl.ds(position * width, count * width)], preferred_element_type=F32
        )

    pair = 2 if row_count % 2 == 0 else 1
    for base in range(0, row_count, pair):
        total = product(turned[1], base + 1, pair)
        if base == 0:
            above = product(top, 0, 1)
            if pair == 2:
                above = jnp.concatenate([above, product(turned[2], 1, 1)], axis=1)
        else:
            above = product(turned[2], base, pair)
        if base + pair == row_count:
            below = product(bottom, row_count + 1, 1)
            if pair == 2:
                below = jnp.concatenate([product(turned[0], row_count, 1), below], axis=1)
        else:
            below = product(turned[0], base + 2, pair)
        total = total + above + below
        for offset in range(pair):
            value = total[:, offset * width : (offset + 1) * width]
            wide[pl.ds(base + offset, channels, stride=row_count), :] = value
    size = (channels - hid) * row_count
    inputs_out[...] = wide[0:size, :].reshape(inputs_out.shape).astype(BF16)
    hidden_out[...] = wide[size:, :].reshape(hidden_out.shape).astype(BF16)


def body(
    place,
    inputs_below,
    hidden_prev,
    cell_prev,
    kernel_weights,
    gate_bias,
    readout,
    target_field,
    land_mask,
    fire_mask,
    hidden_grad,
):
    hid, row_count, width = hidden_prev.shape
    gate_count, channels = kernel_weights.shape[1:]
    cells = row_count * width
    halo_cells = (row_count + 2) * width
    scaling = 1.0 / math.sqrt(cells * place.lat * place.lon)
    bind = functools.partial
    inner_rows, outer_rows = place.pairs(place.inner_rows), place.pairs(place.outer_rows)
    inner_columns = place.pairs(place.inner_columns)
    outer_columns = place.pairs(place.outer_columns)
    flat = sds((hid * row_count, width), F32)

    inner, outer, wide = call(
        pack_kernel,
        (
            sds((channels, width), BF16),
            sds((channels, width), BF16),
            sds((channels * row_count, width), F32),
        ),
        [
            pltpu.VMEM(inputs_below.shape, BF16),
            pltpu.VMEM(hidden_prev.shape, BF16),
            pltpu.SemaphoreType.DMA((2,)),
        ],
        remote=2,
        moved=4 * channels * cells,
    )(inputs_below, hidden_prev)
    inner, outer = permuted(inner, inner_rows), permuted(outer, outer_rows)
    (
        rows,
        columns,
        cell_here,
        weights_here,
        hidden_grad_here,
        target_here,
        land_here,
        fire_here,
        bias_wide,
        readout_wide,
    ) = call(
        prepare_kernel,
        (
            sds((row_count, channels, width), BF16),
            sds((channels, width), F32),
            flat,
            sds(kernel_weights.shape, BF16),
            flat,
            sds(target_field.shape, F32),
            sds(land_mask.shape, jnp.int32),
            sds(fire_mask.shape, jnp.int32),
            sds((gate_count, width), F32),
            sds((hid, width), F32),
        ),
        [
            pltpu.VMEM(hidden_grad.shape, BF16),
            pltpu.VMEM(gate_bias.shape, F32),
            pltpu.VMEM(readout.shape, F32),
            pltpu.SemaphoreType.DMA((8,)),
        ],
        remote=8,
        moved=6_000_000,
    )(
        wide,
        cell_prev.reshape(hid * row_count, width),
        kernel_weights,
        hidden_grad,
        target_field,
        land_mask,
        fire_mask,
        gate_bias,
        readout,
    )
    columns = call(bind(columns_kernel, row_count), sds((channels, width), BF16))(
        columns, inner, outer
    )

    sizes = [place.rows >> (phase + 1) for phase in range(len(place.bits))]
    (
        hidden_next,
        cell_next,
        grad_cell,
        pre,
        pre_inner,
        pre_outer,
        pre_columns,
        send,
        keep,
        bias,
    ) = call(
        bind(gates_kernel, place),
        (
            sds((hid, row_count, width), BF16),
            flat,
            flat,
            sds((gate_count, cells), BF16),
            sds((gate_count, width), BF16),
            sds((gate_count, width), BF16),
            sds((gate_count, width), BF16),
            sds((BIAS_ROWS + sizes[0], channels), BF16),
            sds((sizes[0], channels), F32),
            sds((8, channels), F32),
        ),
        [
            pltpu.VMEM((3 * channels, halo_cells), BF16),
            pltpu.VMEM((hid * row_count, width), F32),
            pltpu.VMEM((place.rows, channels), F32),
        ],
        flops=4 * 9 * gate_count * channels * cells,
        moved=4_000_000,
        transcendentals=5 * hid * cells,
    )(
        rows,
        inner,
        outer,
        permuted(columns, inner_columns),
        permuted(columns, outer_columns),
        cell_here,
        weights_here,
        hidden_grad_here,
        target_here,
        land_here,
        fire_here,
        bias_wide,
        readout_wide,
    )

    pre_inner, pre_outer = permuted(pre_inner, inner_rows), permuted(pre_outer, outer_rows)
    pre_columns = call(bind(columns_kernel, row_count), sds((gate_count, width), BF16))(
        pre_columns, pre_inner, pre_outer
    )
    grad_inputs, grad_hidden, field_done = call(
        bind(field_kernel, place),
        (
            sds((channels - hid, row_count, width), BF16),
            sds((hid, row_count, width), BF16),
            sds((8, width), F32),
        ),
        [
            pltpu.VMEM((3 * gate_count, halo_cells), BF16),
            pltpu.VMEM((3, channels, 3 * gate_count), BF16),
            pltpu.VMEM((channels * row_count, width), F32),
        ],
        flops=2 * 9 * gate_count * channels * cells,
        moved=2_000_000,
    )(
        pre,
        pre_inner,
        pre_outer,
        permuted(pre_columns, inner_columns),
        permuted(pre_columns, outer_columns),
        weights_here,
    )

    last = len(place.bits) - 1
    after = [target_here, pre_columns, target_here, field_done]
    after += [target_here] * last
    for phase in range(last + 1):
        received = permuted(send, place.phase_pairs(phase))
        kernel = bind(halve_kernel, place, phase, scaling)
        if phase < last:
            size = sizes[phase + 1]
            send, keep, bias = call(
                kernel,
                (
                    sds((BIAS_ROWS + size, channels), BF16),
                    sds((size, channels), F32),
                    sds((8, channels), F32),
                ),
                [pltpu.VMEM((2 * size, channels), F32)],
            )(keep, bias, received, after[phase])
        else:
            block = call(kernel, (sds((BIAS_ROWS + sizes[last], channels), BF16),))(
                keep, bias, received, after[phase]
            )[0]
    for phase in range(last, 0, -1):
        received = permuted(block, place.phase_pairs(phase))
        block = call(
            bind(double_kernel, place, phase),
            sds((BIAS_ROWS + sizes[phase - 1], channels), BF16),
        )(block, received)
    grad_kernel, grad_bias = call(
        bind(finish_kernel, place),
        (sds((place.rows, channels), F32), sds((8, channels), F32)),
    )(block, permuted(block, place.phase_pairs(0)))
    shape = hidden_prev.shape
    return (
        hidden_next,
        cell_next.reshape(shape),
        grad_inputs,
        grad_hidden,
        grad_cell.reshape(shape),
        grad_kernel[: 9 * gate_count].reshape(kernel_weights.shape),
        grad_bias[: gate_count // channels].reshape(gate_count),
    )


def solution(mesh):
    lat_count, lon_count = mesh.shape["lat"], mesh.shape["lon"]
    split = Mesh(mesh.devices.reshape(lat_count // 2, 2, lon_count), AXES)
    field = P(None, ("band", "core"), "lon")
    flat = P(("band", "core"), "lon")

    def run(*args):
        place = Layout(lat_count, lon_count, args[3].shape[0] * args[3].shape[1])
        return jax.shard_map(
            functools.partial(body, place),
            mesh=split,
            in_specs=(field, field, field, P(), P(), P(), flat, flat, flat, field),
            out_specs=(field, field, field, field, field, P(), P()),
            check_vma=False,
        )(*args)

    return run
```

profile of v0, /device:TPU:0, one launch (start us, length us, event | category | flops | bytes accessed | tf_op | source)
XLA Modules:
  0.0 65.0 jit_solution(11109191063539834846)
XLA Ops:
  0.6 1.0 %shard_map.153 = (bf16[128,128]{1,0:T(8,128)(2,1)S(1)}, bf16[128,128]{1,0:T(8,128)(2,1)S(1)}, f32[1024,128]{1,0:T(8,128)S(1)}) custom-call(bf16[64,8,128]{2,1,0:T(8,128)(2,1)} %below.1, bf16[64,8,128]{2,1,0:T(8,128)(2,1)} %hidden.1), custom_call_target="tpu_custom_call" | custom-call | bytes 524288 | tf_op jit(solution)/shard_map/pallas_call | solution.py:29
  1.7 0.5 collective-permute-start
  2.2 3.7 %collective-permute-start.1 = (bf16[128,128]{1,0:T(8,128)(2,1)S(1)}, bf16[128,128]{1,0:T(8,128)(2,1)S(1)}, u32[]{:S(2)}, u32[]{:S(2)}) collective-permute-start(bf16[128,128]{1,0:T(8,128)(2,1)S(1)} %get-tuple-element.50), channel_id=1, source_target_pairs={{0,4},{1,5},{2,6},{3,7},{4,0},{5,1},{6,2},{7,3},{8,16},{9,17},{10,... | collective-permute-start | bytes 98312 | tf_op jit(solution)/shard_map/ppermute | solution.py:92
  5.8 1.5 %shard_map.154 = (bf16[8,128,128]{2,1,0:T(8,128)(2,1)S(1)}, f32[128,128]{1,0:T(8,128)S(1)}, f32[512,128]{1,0:T(8,128)S(1)}, bf16[9,256,128]{2,1,0:T(8,128)(2,1)S...) custom-call(f32[1024,128]{1,0:T(8,128)S(1)} %get-tuple-element.47.wi, ...), custom_call_target="tpu_custom_call" | custom-call | bytes 6000000 | tf_op jit(solution)/shard_map/pallas_call | solution.py:29
  7.4 0.0 collective-permute-done.inner.inner_row
  7.4 0.4 collective-permute-done.1.outer.outer_row
  7.7 0.1 shard_map.155
  7.8 5.2 %collective-permute-start.3 = (bf16[128,128]{1,0:T(8,128)(2,1)S(1)}, bf16[128,128]{1,0:T(8,128)(2,1)S(1)}, u32[]{:S(2)}, u32[]{:S(2)}) collective-permute-start(bf16[128,128]{1,0:T(8,128)(2,1)S(1)} %shard_map.155), channel_id=1, source_target_pairs={{0,7},{1,2},{2,1},{3,4},{4,3},{5,6},{6,5},{7,0},{8,15},{9,10},{10,... | collective-permute-start | bytes 98312 | tf_op jit(solution)/shard_map/ppermute | solution.py:92
  13.0 0.0 collective-permute-start.2
  13.0 1.9 %collective-permute-done.3.outer_column = bf16[128,128]{1,0:T(8,128)(2,1)S(1)} collective-permute-done((bf16[128,128]{1,0:T(8,128)(2,1)S(1)}, bf16[128,128]{1,0:T(8,128)(2,1)S(1)}, u32[]{:S(2)}, u32[]{:S(2)}) %collective-permute-start.3) | collective-permute-done | bytes 32800 | tf_op jit(solution)/shard_map/ppermute | solution.py:92
  14.9 2.0 %collective-permute-done.2.inner_column = bf16[128,128]{1,0:T(8,128)(2,1)S(1)} collective-permute-done((bf16[128,128]{1,0:T(8,128)(2,1)S(1)}, bf16[128,128]{1,0:T(8,128)(2,1)S(1)}, u32[]{:S(2)}, u32[]{:S(2)}) %collective-permute-start.2) | collective-permute-done | bytes 32800 | tf_op jit(solution)/shard_map/ppermute | solution.py:92
  16.9 2.6 %shard_map.156 = (bf16[64,8,128]{2,1,0:T(8,128)(2,1)}, f32[512,128]{1,0:T(8,128)}, f32[512,128]{1,0:T(8,128)}, bf16[256,1024]{1,0:T(8,128)(2,1)S(1)}, bf16[256,1...) custom-call(bf16[8,128,128]{2,1,0:T(8,128)(2,1)S(1)} %get-tuple-elem, ...), custom_call_target="tpu_custom_call" | custom-call | flops 1207959552 | bytes 4000000 | tf_op jit(solution)/shard_map/pallas_call | solution.py:29
  19.6 0.0 collective-permute-start.8
  19.6 1.6 %collective-permute-done.8.received = bf16[1168,128]{1,0:T(8,128)(2,1)S(1)} collective-permute-done((bf16[1168,128]{1,0:T(8,128)(2,1)S(1)}, bf16[1168,128]{1,0:T(8,128)(2,1)S(1)}, u32[]{:S(2)}, u32[]{:S(2)}) %collective-permute-start.8) | collective-permute-done | bytes 299040 | tf_op jit(solution)/shard_map/ppermute | solution.py:92
  21.2 0.1 shard_map.159
  21.3 0.1 collective-permute-start.9
  21.3 0.2 collective-permute-start.4
  21.5 0.0 collective-permute-start.5
  21.6 1.1 %collective-permute-done.4.inner.inner_row = bf16[256,128]{1,0:T(8,128)(2,1)S(1)} collective-permute-done((bf16[256,128]{1,0:T(8,128)(2,1)S(1)}, bf16[256,128]{1,0:T(8,128)(2,1)S(1)}, u32[]{:S(2)}, u32[]{:S(2)}) %collective-permute-start.4) | collective-permute-done | bytes 65568 | tf_op jit(solution)/shard_map/ppermute | solution.py:92
  22.7 4.0 %collective-permute-done.5.outer.outer_row = bf16[256,128]{1,0:T(8,128)(2,1)S(1)} collective-permute-done((bf16[256,128]{1,0:T(8,128)(2,1)S(1)}, bf16[256,128]{1,0:T(8,128)(2,1)S(1)}, u32[]{:S(2)}, u32[]{:S(2)}) %collective-permute-start.5) | collective-permute-done | bytes 65568 | tf_op jit(solution)/shard_map/ppermute | solution.py:92
  26.7 0.1 shard_map.157.after
  26.8 0.5 collective-permute-done.9.received
  27.3 0.1 shard_map.160
  27.4 0.3 collective-permute-start.10
  27.7 2.5 %collective-permute-start.7 = (bf16[256,128]{1,0:T(8,128)(2,1)S(1)}, bf16[256,128]{1,0:T(8,128)(2,1)S(1)}, u32[]{:S(2)}, u32[]{:S(2)}) collective-permute-start(bf16[256,128]{1,0:T(8,128)(2,1)S(1)} %shard_map.157.after), channel_id=1, source_target_pairs={{0,7},{1,2},{2,1},{3,4},{4,3},{5,6},{6,5},{7,0},{8,15},{9,10},{10,... | collective-permute-start | bytes 196616 | tf_op jit(solution)/shard_map/ppermute | solution.py:92
  30.2 0.0 collective-permute-start.6
  30.2 2.1 %collective-permute-done.10.received = bf16[304,128]{1,0:T(8,128)(2,1)S(1)} collective-permute-done((bf16[304,128]{1,0:T(8,128)(2,1)S(1)}, bf16[304,128]{1,0:T(8,128)(2,1)S(1)}, u32[]{:S(2)}, u32[]{:S(2)}) %collective-permute-start.10) | collective-permute-done | bytes 77856 | tf_op jit(solution)/shard_map/ppermute | solution.py:92
  32.4 0.1 collective-permute-start.11
  32.5 2.5 %collective-permute-done.7.outer_column = bf16[256,128]{1,0:T(8,128)(2,1)S(1)} collective-permute-done((bf16[256,128]{1,0:T(8,128)(2,1)S(1)}, bf16[256,128]{1,0:T(8,128)(2,1)S(1)}, u32[]{:S(2)}, u32[]{:S(2)}) %collective-permute-start.7) | collective-permute-done | bytes 65568 | tf_op jit(solution)/shard_map/ppermute | solution.py:92
  35.0 1.0 %collective-permute-done.6.inner_column = bf16[256,128]{1,0:T(8,128)(2,1)S(1)} collective-permute-done((bf16[256,128]{1,0:T(8,128)(2,1)S(1)}, bf16[256,128]{1,0:T(8,128)(2,1)S(1)}, u32[]{:S(2)}, u32[]{:S(2)}) %collective-permute-start.6) | collective-permute-done | bytes 65568 | tf_op jit(solution)/shard_map/ppermute | solution.py:92
  36.0 2.1 %shard_map.158 = (bf16[64,8,128]{2,1,0:T(8,128)(2,1)}, bf16[64,8,128]{2,1,0:T(8,128)(2,1)}, f32[8,128]{1,0:T(8,128)S(1)}) custom-call(bf16[256,1024]{1,0:T(8,128)(2,1)S(1)} %get-tuple-element.62.pre, bf16[256,128]{1,0:T(8,128)(2,1)S(1)} %collective-permute-done.4.inner.inner_row, bf16[256,128]{1,0:T(8,128)(2,1)S(1)} %collective-permute-done.5.outer.outer_row, ...), custom_call_target="tpu_custom_call" | custom-call | flops 603979776 | bytes 2000000 | tf_op jit(solution)/shard_map/pallas_call | solution.py:29
  38.1 0.0 collective-permute-done.11.received
  38.1 0.1 collective-permute-start.12
  38.2 4.7 %collective-permute-done.12.received = bf16[88,128]{1,0:T(8,128)(2,1)S(1)} collective-permute-done((bf16[88,128]{1,0:T(8,128)(2,1)S(1)}, bf16[88,128]{1,0:T(8,128)(2,1)S(1)}, u32[]{:S(2)}, u32[]{:S(2)}) %collective-permute-start.12) | collective-permute-done | bytes 22560 | tf_op jit(solution)/shard_map/ppermute | solution.py:92
  42.9 0.2 collective-permute-start.13
  43.1 4.6 %collective-permute-done.13.received = bf16[88,128]{1,0:T(8,128)(2,1)S(1)} collective-permute-done((bf16[88,128]{1,0:T(8,128)(2,1)S(1)}, bf16[88,128]{1,0:T(8,128)(2,1)S(1)}, u32[]{:S(2)}, u32[]{:S(2)}) %collective-permute-start.13) | collective-permute-done | bytes 22560 | tf_op jit(solution)/shard_map/ppermute | solution.py:92
  47.7 0.1 collective-permute-start.14
  47.8 4.0 %collective-permute-done.14.received = bf16[160,128]{1,0:T(8,128)(2,1)S(1)} collective-permute-done((bf16[160,128]{1,0:T(8,128)(2,1)S(1)}, bf16[160,128]{1,0:T(8,128)(2,1)S(1)}, u32[]{:S(2)}, u32[]{:S(2)}) %collective-permute-start.14) | collective-permute-done | bytes 40992 | tf_op jit(solution)/shard_map/ppermute | solution.py:92
  51.8 0.2 collective-permute-start.15
  52.0 4.3 %collective-permute-done.15.received = bf16[304,128]{1,0:T(8,128)(2,1)S(1)} collective-permute-done((bf16[304,128]{1,0:T(8,128)(2,1)S(1)}, bf16[304,128]{1,0:T(8,128)(2,1)S(1)}, u32[]{:S(2)}, u32[]{:S(2)}) %collective-permute-start.15) | collective-permute-done | bytes 77856 | tf_op jit(solution)/shard_map/ppermute | solution.py:92
  56.3 0.4 collective-permute-start.16
  56.7 4.9 %collective-permute-done.16.received = bf16[592,128]{1,0:T(8,128)(2,1)S(1)} collective-permute-done((bf16[592,128]{1,0:T(8,128)(2,1)S(1)}, bf16[592,128]{1,0:T(8,128)(2,1)S(1)}, u32[]{:S(2)}, u32[]{:S(2)}) %collective-permute-start.16) | collective-permute-done | bytes 151584 | tf_op jit(solution)/shard_map/ppermute | solution.py:92
  61.6 0.1 shard_map.167.own
  61.7 0.1 collective-permute-start.17
  61.7 1.6 %collective-permute-done.17.received = bf16[1168,128]{1,0:T(8,128)(2,1)S(1)} collective-permute-done((bf16[1168,128]{1,0:T(8,128)(2,1)S(1)}, bf16[1168,128]{1,0:T(8,128)(2,1)S(1)}, u32[]{:S(2)}, u32[]{:S(2)}) %collective-permute-start.17) | collective-permute-done | bytes 299040 | tf_op jit(solution)/shard_map/ppermute | solution.py:92
  63.3 1.1 %shard_map.168 = (f32[2304,128]{1,0:T(8,128)}, f32[8,128]{1,0:T(8,128)S(1)}) custom-call(bf16[1168,128]{1,0:T(8,128)(2,1)S(1)} %shard_map.167.own, bf16[1168,128]{1,0:T(8,128)(2,1)S(1)} %collective-permute-done.17.received), custom_call_target="tpu_custom_call" | custom-call | tf_op jit(solution)/shard_map/pallas_call | solution.py:29
  64.4 0.6 slice_bitcast_fusion
  (6 shorter events, 0.1 us)
Async XLA Ops:
  1.7 5.7 %collective-permute-start = (bf16[128,128]{1,0:T(8,128)(2,1)S(1)}, bf16[128,128]{1,0:T(8,128)(2,1)S(1)}, u32[]{:S(2)}, u32[]{:S(2)}) collective-permute-start(bf16[128,128]{1,0:T(8,128)(2,1)S(1)} %get-tuple-element.49), channel_id=1, source_target_pairs={{0,8},{1,9},{2,10},{3,11},{4,12},{5,13},{6,14},{7,15},{8,0},{9,1},... | collective-permute-start | bytes 98312 | tf_op jit(solution)/shard_map/ppermute | solution.py:92
  2.2 5.6 %collective-permute-start.1 = (bf16[128,128]{1,0:T(8,128)(2,1)S(1)}, bf16[128,128]{1,0:T(8,128)(2,1)S(1)}, u32[]{:S(2)}, u32[]{:S(2)}) collective-permute-start(bf16[128,128]{1,0:T(8,128)(2,1)S(1)} %get-tuple-element.50), channel_id=1, source_target_pairs={{0,4},{1,5},{2,6},{3,7},{4,0},{5,1},{6,2},{7,3},{8,16},{9,17},{10,... | collective-permute-start | bytes 98312 | tf_op jit(solution)/shard_map/ppermute | solution.py:92
  7.8 7.1 %collective-permute-start.3 = (bf16[128,128]{1,0:T(8,128)(2,1)S(1)}, bf16[128,128]{1,0:T(8,128)(2,1)S(1)}, u32[]{:S(2)}, u32[]{:S(2)}) collective-permute-start(bf16[128,128]{1,0:T(8,128)(2,1)S(1)} %shard_map.155), channel_id=1, source_target_pairs={{0,7},{1,2},{2,1},{3,4},{4,3},{5,6},{6,5},{7,0},{8,15},{9,10},{10,... | collective-permute-start | bytes 98312 | tf_op jit(solution)/shard_map/ppermute | solution.py:92
  13.0 3.9 %collective-permute-start.2 = (bf16[128,128]{1,0:T(8,128)(2,1)S(1)}, bf16[128,128]{1,0:T(8,128)(2,1)S(1)}, u32[]{:S(2)}, u32[]{:S(2)}) collective-permute-start(bf16[128,128]{1,0:T(8,128)(2,1)S(1)} %shard_map.155), channel_id=1, source_target_pairs={{0,1},{1,0},{2,3},{3,2},{4,5},{5,4},{6,7},{7,6},{8,9},{9,8},{10,11... | collective-permute-start | bytes 98312 | tf_op jit(solution)/shard_map/ppermute | solution.py:92
  19.6 1.6 %collective-permute-start.8 = (bf16[1168,128]{1,0:T(8,128)(2,1)S(1)}, bf16[1168,128]{1,0:T(8,128)(2,1)S(1)}, u32[]{:S(2)}, u32[]{:S(2)}) collective-permute-start(bf16[1168,128]{1,0:T(8,128)(2,1)S(1)} %get-tuple-element.71), channel_id=1, source_target_pairs={{0,8},{1,9},{2,10},{3,11},{4,12},{5,13},{6,14},{7,15},{8,0},{9,1},... | collective-permute-start | bytes 897032 | tf_op jit(solution)/shard_map/ppermute | solution.py:92
  21.3 6.0 %collective-permute-start.9 = (bf16[592,128]{1,0:T(8,128)(2,1)S(1)}, bf16[592,128]{1,0:T(8,128)(2,1)S(1)}, u32[]{:S(2)}, u32[]{:S(2)}) collective-permute-start(bf16[592,128]{1,0:T(8,128)(2,1)S(1)} %get-tuple-element.74), channel_id=1, source_target_pairs={{0,16},{1,17},{2,18},{3,19},{4,20},{5,21},{6,22},{7,23},{8,24},{9,... | collective-permute-start | bytes 454664 | tf_op jit(solution)/shard_map/ppermute | solution.py:92
  21.3 1.3 %collective-permute-start.4 = (bf16[256,128]{1,0:T(8,128)(2,1)S(1)}, bf16[256,128]{1,0:T(8,128)(2,1)S(1)}, u32[]{:S(2)}, u32[]{:S(2)}) collective-permute-start(bf16[256,128]{1,0:T(8,128)(2,1)S(1)} %get-tuple-element.63), channel_id=1, source_target_pairs={{0,8},{1,9},{2,10},{3,11},{4,12},{5,13},{6,14},{7,15},{8,0},{9,1},... | collective-permute-start | bytes 196616 | tf_op jit(solution)/shard_map/ppermute | solution.py:92
  21.5 5.2 %collective-permute-start.5 = (bf16[256,128]{1,0:T(8,128)(2,1)S(1)}, bf16[256,128]{1,0:T(8,128)(2,1)S(1)}, u32[]{:S(2)}, u32[]{:S(2)}) collective-permute-start(bf16[256,128]{1,0:T(8,128)(2,1)S(1)} %get-tuple-element.64), channel_id=1, source_target_pairs={{0,4},{1,5},{2,6},{3,7},{4,0},{5,1},{6,2},{7,3},{8,16},{9,17},{10,... | collective-permute-start | bytes 196616 | tf_op jit(solution)/shard_map/ppermute | solution.py:92
  27.4 5.0 %collective-permute-start.10 = (bf16[304,128]{1,0:T(8,128)(2,1)S(1)}, bf16[304,128]{1,0:T(8,128)(2,1)S(1)}, u32[]{:S(2)}, u32[]{:S(2)}) collective-permute-start(bf16[304,128]{1,0:T(8,128)(2,1)S(1)} %get-tuple-element.77), channel_id=1, source_target_pairs={{0,1},{1,0},{2,3},{3,2},{4,5},{5,4},{6,7},{7,6},{8,9},{9,8},{10,11... | collective-permute-start | bytes 233480 | tf_op jit(solution)/shard_map/ppermute | solution.py:92
  27.7 7.3 %collective-permute-start.7 = (bf16[256,128]{1,0:T(8,128)(2,1)S(1)}, bf16[256,128]{1,0:T(8,128)(2,1)S(1)}, u32[]{:S(2)}, u32[]{:S(2)}) collective-permute-start(bf16[256,128]{1,0:T(8,128)(2,1)S(1)} %shard_map.157.after), channel_id=1, source_target_pairs={{0,7},{1,2},{2,1},{3,4},{4,3},{5,6},{6,5},{7,0},{8,15},{9,10},{10,... | collective-permute-start | bytes 196616 | tf_op jit(solution)/shard_map/ppermute | solution.py:92
  30.2 5.8 %collective-permute-start.6 = (bf16[256,128]{1,0:T(8,128)(2,1)S(1)}, bf16[256,128]{1,0:T(8,128)(2,1)S(1)}, u32[]{:S(2)}, u32[]{:S(2)}) collective-permute-start(bf16[256,128]{1,0:T(8,128)(2,1)S(1)} %shard_map.157.after), channel_id=1, source_target_pairs={{0,1},{1,0},{2,3},{3,2},{4,5},{5,4},{6,7},{7,6},{8,9},{9,8},{10,11... | collective-permute-start | bytes 196616 | tf_op jit(solution)/shard_map/ppermute | solution.py:92
  32.4 5.7 %collective-permute-start.11 = (bf16[160,128]{1,0:T(8,128)(2,1)S(1)}, bf16[160,128]{1,0:T(8,128)(2,1)S(1)}, u32[]{:S(2)}, u32[]{:S(2)}) collective-permute-start(bf16[160,128]{1,0:T(8,128)(2,1)S(1)} %get-tuple-element.80), channel_id=1, source_target_pairs={{0,2},{1,3},{2,0},{3,1},{4,6},{5,7},{6,4},{7,5},{8,10},{9,11},{10,... | collective-permute-start | bytes 122888 | tf_op jit(solution)/shard_map/ppermute | solution.py:92
  38.1 4.8 %collective-permute-start.12 = (bf16[88,128]{1,0:T(8,128)(2,1)S(1)}, bf16[88,128]{1,0:T(8,128)(2,1)S(1)}, u32[]{:S(2)}, u32[]{:S(2)}) collective-permute-start(bf16[88,128]{1,0:T(8,128)(2,1)S(1)} %get-tuple-element.84), channel_id=1, source_target_pairs={{0,4},{1,5},{2,6},{3,7},{4,0},{5,1},{6,2},{7,3},{8,12},{9,13},{10,... | collective-permute-start | bytes 67592 | tf_op jit(solution)/shard_map/ppermute | solution.py:92
  42.9 4.8 %collective-permute-start.13 = (bf16[88,128]{1,0:T(8,128)(2,1)S(1)}, bf16[88,128]{1,0:T(8,128)(2,1)S(1)}, u32[]{:S(2)}, u32[]{:S(2)}) collective-permute-start(bf16[88,128]{1,0:T(8,128)(2,1)S(1)} %shard_map.163.own), channel_id=1, source_target_pairs={{0,4},{1,5},{2,6},{3,7},{4,0},{5,1},{6,2},{7,3},{8,12},{9,13},{10,... | collective-permute-start | bytes 67592 | tf_op jit(solution)/shard_map/ppermute | solution.py:92
  47.7 4.1 %collective-permute-start.14 = (bf16[160,128]{1,0:T(8,128)(2,1)S(1)}, bf16[160,128]{1,0:T(8,128)(2,1)S(1)}, u32[]{:S(2)}, u32[]{:S(2)}) collective-permute-start(bf16[160,128]{1,0:T(8,128)(2,1)S(1)} %shard_map.164.own), channel_id=1, source_target_pairs={{0,2},{1,3},{2,0},{3,1},{4,6},{5,7},{6,4},{7,5},{8,10},{9,11},{10,... | collective-permute-start | bytes 122888 | tf_op jit(solution)/shard_map/ppermute | solution.py:92
  51.8 4.5 %collective-permute-start.15 = (bf16[304,128]{1,0:T(8,128)(2,1)S(1)}, bf16[304,128]{1,0:T(8,128)(2,1)S(1)}, u32[]{:S(2)}, u32[]{:S(2)}) collective-permute-start(bf16[304,128]{1,0:T(8,128)(2,1)S(1)} %shard_map.165.own), channel_id=1, source_target_pairs={{0,1},{1,0},{2,3},{3,2},{4,5},{5,4},{6,7},{7,6},{8,9},{9,8},{10,11... | collective-permute-start | bytes 233480 | tf_op jit(solution)/shard_map/ppermute | solution.py:92
  56.3 5.3 %collective-permute-start.16 = (bf16[592,128]{1,0:T(8,128)(2,1)S(1)}, bf16[592,128]{1,0:T(8,128)(2,1)S(1)}, u32[]{:S(2)}, u32[]{:S(2)}) collective-permute-start(bf16[592,128]{1,0:T(8,128)(2,1)S(1)} %shard_map.166.own), channel_id=1, source_target_pairs={{0,16},{1,17},{2,18},{3,19},{4,20},{5,21},{6,22},{7,23},{8,24},{9,... | collective-permute-start | bytes 454664 | tf_op jit(solution)/shard_map/ppermute | solution.py:92
  61.7 1.7 %collective-permute-start.17 = (bf16[1168,128]{1,0:T(8,128)(2,1)S(1)}, bf16[1168,128]{1,0:T(8,128)(2,1)S(1)}, u32[]{:S(2)}, u32[]{:S(2)}) collective-permute-start(bf16[1168,128]{1,0:T(8,128)(2,1)S(1)} %shard_map.167.own), channel_id=1, source_target_pairs={{0,8},{1,9},{2,10},{3,11},{4,12},{5,13},{6,14},{7,15},{8,0},{9,1},... | collective-permute-start | bytes 897032 | tf_op jit(solution)/shard_map/ppermute | solution.py:92
where the time goes:
time: 65.1 us; the launch traced here: 65 us
  waiting for transfers between devices  41.1 us (63%)
  starting transfers between devices  13.5 us (21%)
  Pallas kernels  8.95 us (14%)
  between operations  0.78 us (1%)
    ppermute x18, waiting for transfers between devices, permuted(): return lax.ppermute(value, AXES, pairs)  41.1 us
    ppermute x18, starting transfers between devices, permuted(): return lax.ppermute(value, AXES, pairs)  13.5 us
    pallas_call x16, Pallas kernels, run(): pl.pallas_call(kernel, out_shape=out_shape, in_specs=[VMEM] * near + [HBM...  8.95 us
  transfers between devices with their start and end apart: 18, of which 16 were waited for; matrix products, arithmetic and copies ran while one was open for 0% of the time, Pallas kernels for 6%

commit v1 on v0

--- a/solution.py
+++ b/solution.py
@@ -22,7 +22,21 @@
     return jax.ShapeDtypeStruct(shape, dtype)
 
 
-def call(kernel, out_shape, scratch=(), remote=0, flops=0, moved=0, transcendentals=0):
+def call(
+    kernel,
+    out_shape,
+    scratch=(),
+    remote=0,
+    leaving=0,
+    aliases=None,
+    flops=0,
+    moved=0,
+    transcendentals=0,
+):
+    several = isinstance(out_shape, tuple)
+    shapes = out_shape if several else (out_shape,)
+    out_specs = tuple([HBM] * leaving + [VMEM] * (len(shapes) - leaving))
+
     def run(*args):
         near = len(args) - remote
         far = [pltpu.with_memory_space_constraint(arg, pltpu.HBM) for arg in args[near:]]
@@ -30,7 +44,8 @@
             kernel,
             out_shape=out_shape,
             in_specs=[VMEM] * near + [HBM] * remote,
-            out_specs=jax.tree.map(lambda _: VMEM, out_shape),
+            out_specs=out_specs if several else out_specs[0],
+            input_output_aliases=aliases or {},
             scratch_shapes=list(scratch),
             cost_estimate=pl.CostEstimate(
                 flops=flops, bytes_accessed=moved, transcendentals=transcendentals
@@ -45,18 +60,30 @@
     def __init__(self, lat_count, lon_count, kernel_rows):
         self.lat, self.lon = lat_count, lon_count
         self.half = lon_count // 2
-        devices = lat_count * lon_count
-        self.rows = -(-kernel_rows // (devices * 8)) * devices * 8
-        self.bits = [("lat", 1 << k) for k in range(lat_count.bit_length() - 1)]
-        self.bits += [("lon", 1 << k) for k in range(lon_count.bit_length() - 1)]
+        scatter = [("lat", 1 << k) for k in range(1, lat_count.bit_length() - 1)]
+        lon_bits = [("lon", 1 << k) for k in range(lon_count.bit_length() - 1)]
+        scatter += lon_bits[:-2]
+        whole = lon_bits[-2:]
+        self.scatter_phases = 1 + len(scatter)
+        self.orders = (
+            [("lat", 1)] + scatter + whole,
+            [("lat", 1)] + scatter[::-1] + whole[::-1],
+        )
+        step = 8 << self.scatter_phases
+        self.rows = -(-kernel_rows // step) * step
+        self.sizes = [self.rows >> (phase + 1) for phase in range(self.scatter_phases)]
 
     def position(self):
         return 2 * lax.axis_index("band") + lax.axis_index("core"), lax.axis_index("lon")
 
     def rank(self, phase):
-        axis, bit = self.bits[phase]
         lat, lon = self.position()
-        return ((lat if axis == "lat" else lon) // bit) % 2
+
+        def digit(order):
+            axis, bit = order[phase]
+            return ((lat if axis == "lat" else lon) // bit) % 2
+
+        return jnp.where(lat % 2 == 0, digit(self.orders[0]), digit(self.orders[1]))
 
     def pairs(self, partner):
         result = []
@@ -67,10 +94,11 @@
         return result
 
     def phase_pairs(self, phase):
-        axis, bit = self.bits[phase]
-        if axis == "lat":
-            return self.pairs(lambda lat, lon: (lat ^ bit, lon))
-        return self.pairs(lambda lat, lon: (lat, lon ^ bit))
+        def partner(lat, lon):
+            axis, bit = self.orders[lat % 2][phase]
+            return (lat ^ bit, lon) if axis == "lat" else (lat, lon ^ bit)
+
+        return self.pairs(partner)
 
     def inner_rows(self, lat, lon):
         return lat ^ 1, lon
@@ -235,7 +263,17 @@
 
 def columns_kernel(row_count, columns, inner, outer, out):
     north, south = row_halo(inner, outer)
-    value = edge_columns(north, 0, columns[...].astype(F32))
+    value = edge_columns(north, 0, columns[...])
+    out[...] = edge_columns(south, row_count + 1, value).astype(BF16)
+
+
+def pre_columns_kernel(row_count, pre, inner, outer, out):
+    width = out.shape[1]
+    north, south = row_halo(inner, outer)
+    value = edge_columns(north, 0, jnp.zeros(north.shape, F32))
+    for index in range(row_count):
+        row = pre[:, pl.ds(index * width, width)].astype(F32)
+        value = edge_columns(row, index + 1, value)
     out[...] = edge_columns(south, row_count + 1, value).astype(BF16)
 
 
@@ -272,19 +310,22 @@
     fire,
     bias_wide,
     readout_wide,
-    hidden_out,
-    cell_out,
-    grad_cell_out,
+    hidden_hbm,
+    cell_hbm,
+    grad_cell_hbm,
     pre_out,
     inner_out,
     outer_out,
-    columns_out,
     send_out,
     keep_out,
     bias_out,
     shifted,
     hidden_wide,
+    hidden_low,
+    cell_out,
+    grad_cell_out,
     sums,
+    left,
 ):
     row_count, channels, width = rows_in.shape
     gate_count = weights.shape[1]
@@ -309,7 +350,6 @@
         for a in range(3)
     ]
     bias_total = jnp.zeros((gate_count, width), F32)
-    columns = jnp.zeros((gate_count, width), F32)
     edges = []
     readout = readout_wide[...]
     pair = 2 if row_count % 2 == 0 else 1
@@ -352,13 +392,19 @@
                 axis=0,
             )
             bias_total += pre_grad
-            columns = edge_columns(pre_grad, index + 1, columns)
             pre_out[:, pl.ds(index * width, width)] = pre_grad.astype(BF16)
             if index in (0, row_count - 1):
                 edges.append(pre_grad)
-    hidden_out[...] = hidden_wide[...].reshape(hidden_out.shape).astype(BF16)
+    hidden_low[...] = hidden_wide[...].reshape(hidden_low.shape).astype(BF16)
+    leaving = [
+        pltpu.make_async_copy(source, target, left.at[index])
+        for index, (source, target) in enumerate(
+            ((hidden_low, hidden_hbm), (cell_out, cell_hbm), (grad_cell_out, grad_cell_hbm))
+        )
+    ]
+    for copy in leaving:
+        copy.start()
     row_sends(edges[0], edges[-1], inner_out, outer_out)
-    columns_out[...] = columns.astype(BF16)
 
     for a in range(3):
         product = lax.dot_general(
@@ -383,16 +429,18 @@
     bias_rows = jnp.where(odd, flat[:, channels : 2 * channels], flat[:, 0:channels])
     bias_out[...] = bias_rows
     split_sum(place, 0, bias_rows, sums, place.rows, send_out, keep_out)
-
-
-def halve_kernel(place, phase, scaling, keep, bias, received, after, *outs):
+    for copy in leaving:
+        copy.wait()
+
+
+def halve_kernel(place, phase, keep, bias, received, after, *outs):
     del after
     total = keep[...] + received[BIAS_ROWS:, :].astype(F32)
     bias_total = bias[...] + decode(received[0:BIAS_ROWS, :].astype(F32))
-    if phase == len(place.bits) - 1:
+    if phase == place.scatter_phases - 1:
         (out,) = outs
-        out[0:BIAS_ROWS, :] = encode(bias_total * scaling).astype(BF16)
-        out[BIAS_ROWS:, :] = (total * scaling).astype(BF16)
+        out[0:BIAS_ROWS, :] = encode(bias_total).astype(BF16)
+        out[BIAS_ROWS:, :] = total.astype(BF16)
         return
     send_out, keep_out, bias_out, scratch = outs
     scratch[...] = total
@@ -400,6 +448,14 @@
     split_sum(place, phase + 1, bias_total, scratch, total.shape[0], send_out, keep_out)
 
 
+def add_kernel(scale, own, received, after, out):
+    del after
+    here, there = own[...].astype(F32), received[...].astype(F32)
+    bias = (decode(here[0:BIAS_ROWS]) + decode(there[0:BIAS_ROWS])) * scale
+    out[0:BIAS_ROWS, :] = encode(bias).astype(BF16)
+    out[BIAS_ROWS:, :] = ((here[BIAS_ROWS:] + there[BIAS_ROWS:]) * scale).astype(BF16)
+
+
 def double_kernel(place, phase, own, received, out):
     odd = place.rank(phase) == 1
     here, there = own[...].astype(F32), received[...].astype(F32)
@@ -407,14 +463,29 @@
     out[...] = jnp.concatenate([first, second[BIAS_ROWS:]], axis=0).astype(BF16)
 
 
-def finish_kernel(place, own, received, out, bias_out):
-    odd = place.rank(0) == 1
+def own_half_kernel(place, own, out, wide, left):
     rows = own.shape[0] - BIAS_ROWS
-    here, there = own[...].astype(F32), received[...].astype(F32)
+    wide[...] = own[BIAS_ROWS:, :].astype(F32)
+    at = pl.ds(pl.multiple_of(place.rank(0) * rows, 8), rows)
+    copy = pltpu.make_async_copy(wide, out.at[at, :], left.at[0])
+    copy.start()
+    copy.wait()
+
+
+def other_half_kernel(place, own, received, out_before, out, bias_out, wide, left):
+    del out_before
+    rows = received.shape[0] - BIAS_ROWS
+    wide[...] = received[BIAS_ROWS:, :].astype(F32)
     rank = place.rank(0)
-    out[pl.ds(pl.multiple_of(rank * rows, 8), rows), :] = here[BIAS_ROWS:]
-    out[pl.ds(pl.multiple_of((1 - rank) * rows, 8), rows), :] = there[BIAS_ROWS:]
-    bias_out[...] = decode(pick(odd, there[0:BIAS_ROWS], here[0:BIAS_ROWS]))
+    at = pl.ds(pl.multiple_of((1 - rank) * rows, 8), rows)
+    copy = pltpu.make_async_copy(wide, out.at[at, :], left.at[0])
+    copy.start()
+    here, there = own[0:BIAS_ROWS, :].astype(F32), received[0:BIAS_ROWS, :].astype(F32)
+    bias = decode(pick(rank == 1, there, here))
+    width = bias.shape[1]
+    for index in range(bias_out.shape[0] // width):
+        bias_out[pl.ds(index * width, width)] = bias[index]
+    copy.wait()
 
 
 def field_kernel(
@@ -574,7 +645,7 @@
         columns, inner, outer
     )
 
-    sizes = [place.rows >> (phase + 1) for phase in range(len(place.bits))]
+    sizes = place.sizes
     (
         hidden_next,
         cell_next,
@@ -582,7 +653,6 @@
         pre,
         pre_inner,
         pre_outer,
-        pre_columns,
         send,
         keep,
         bias,
@@ -595,7 +665,6 @@
             sds((gate_count, cells), BF16),
             sds((gate_count, width), BF16),
             sds((gate_count, width), BF16),
-            sds((gate_count, width), BF16),
             sds((BIAS_ROWS + sizes[0], channels), BF16),
             sds((sizes[0], channels), F32),
             sds((8, channels), F32),
@@ -603,8 +672,13 @@
         [
             pltpu.VMEM((3 * channels, halo_cells), BF16),
             pltpu.VMEM((hid * row_count, width), F32),
+            pltpu.VMEM((hid, row_count, width), BF16),
+            pltpu.VMEM((hid * row_count, width), F32),
+            pltpu.VMEM((hid * row_count, width), F32),
             pltpu.VMEM((place.rows, channels), F32),
+            pltpu.SemaphoreType.DMA((3,)),
         ],
+        leaving=3,
         flops=4 * 9 * gate_count * channels * cells,
         moved=4_000_000,
         transcendentals=5 * hid * cells,
@@ -625,8 +699,8 @@
     )
 
     pre_inner, pre_outer = permuted(pre_inner, inner_rows), permuted(pre_outer, outer_rows)
-    pre_columns = call(bind(columns_kernel, row_count), sds((gate_count, width), BF16))(
-        pre_columns, pre_inner, pre_outer
+    pre_columns = call(bind(pre_columns_kernel, row_count), sds((gate_count, width), BF16))(
+        pre, pre_inner, pre_outer
     )
     grad_inputs, grad_hidden, field_done = call(
         bind(field_kernel, place),
@@ -651,12 +725,14 @@
         weights_here,
     )
 
-    last = len(place.bits) - 1
-    after = [target_here, pre_columns, target_here, field_done]
-    after += [target_here] * last
+    last = place.scatter_phases - 1
+    phases = len(place.orders[0])
+    after = [target_here] * phases
+    after[1] = pre_columns
+    after[3] = field_done
     for phase in range(last + 1):
         received = permuted(send, place.phase_pairs(phase))
-        kernel = bind(halve_kernel, place, phase, scaling)
+        kernel = bind(halve_kernel, place, phase)
         if phase < last:
             size = sizes[phase + 1]
             send, keep, bias = call(
@@ -672,16 +748,36 @@
             block = call(kernel, (sds((BIAS_ROWS + sizes[last], channels), BF16),))(
                 keep, bias, received, after[phase]
             )[0]
+    for phase in range(last + 1, phases):
+        received = permuted(block, place.phase_pairs(phase))
+        scale = scaling if phase == phases - 1 else 1.0
+        block = call(bind(add_kernel, scale), sds(block.shape, BF16))(
+            block, received, after[phase]
+        )
     for phase in range(last, 0, -1):
         received = permuted(block, place.phase_pairs(phase))
         block = call(
             bind(double_kernel, place, phase),
             sds((BIAS_ROWS + sizes[phase - 1], channels), BF16),
         )(block, received)
+    received = permuted(block, place.phase_pairs(0))
+    half = [pltpu.VMEM((sizes[0], channels), F32), pltpu.SemaphoreType.DMA((1,))]
+    grad_kernel = call(
+        bind(own_half_kernel, place),
+        (sds((place.rows, channels), F32),),
+        half,
+        leaving=1,
+        moved=6 * sizes[0] * channels,
+    )(block)[0]
     grad_kernel, grad_bias = call(
-        bind(finish_kernel, place),
-        (sds((place.rows, channels), F32), sds((8, channels), F32)),
-    )(block, permuted(block, place.phase_pairs(0)))
+        bind(other_half_kernel, place),
+        (sds((place.rows, channels), F32), sds((gate_count,), F32)),
+        half,
+        remote=1,
+        leaving=1,
+        aliases={2: 0},
+        moved=6 * sizes[0] * channels,
+    )(block, received, grad_kernel)
     shape = hidden_prev.shape
     return (
         hidden_next,
@@ -690,7 +786,7 @@
         grad_hidden,
         grad_cell.reshape(shape),
         grad_kernel[: 9 * gate_count].reshape(kernel_weights.shape),
-        grad_bias[: gate_count // channels].reshape(gate_count),
+        grad_bias,
     )
 
 

time: 65.1 us -> 58 us (0.89)
  waiting for transfers between devices: 41.1 us -> 31.2 us
  starting transfers between devices: 13.5 us -> 15.5 us
  Pallas kernels: 8.95 us -> 10.3 us
    ppermute x18 -> x16, waiting for transfers between devices: 41.1 us -> 31.2 us  [permuted(): return lax.ppermute(value, AXES, pairs)]
    ppermute x18 -> x16, starting transfers between devices: 13.5 us -> 15.5 us  [permuted(): return lax.ppermute(value, AXES, pairs)]
    pallas_call x16 -> x15, Pallas kernels: 8.95 us -> 10.3 us  [run(): pl.pallas_call(kernel, out_shape=out_shape, in_specs=[VMEM] * near + [HBM...]
  transfers between devices with their start and end apart: 18 -> 16, of which waited for: 16 -> 13; matrix products, arithmetic and copies ran while one was open for 0% -> 0% of each run, Pallas kernels for 6% -> 8%
where the time goes in v1:
time: 58 us; the launch traced here: 57.8 us
  waiting for transfers between devices  31.2 us (54%)
  starting transfers between devices  15.5 us (27%)
  Pallas kernels  10.3 us (18%)
  between operations  0.78 us (1%)
    ppermute x16, waiting for transfers between devices, permuted(): return lax.ppermute(value, AXES, pairs)  31.2 us
    ppermute x16, starting transfers between devices, permuted(): return lax.ppermute(value, AXES, pairs)  15.5 us
    pallas_call x15, Pallas kernels, run(): pl.pallas_call(kernel, out_shape=out_shape, in_specs=[VMEM] * near + [HBM...  10.3 us
  transfers between devices with their start and end apart: 16, of which 13 were waited for; matrix products, arithmetic and copies ran while one was open for 0% of the time, Pallas kernels for 8%

profile of v1, /device:TPU:0, one launch (start us, length us, event | category | flops | bytes accessed | tf_op | source)
XLA Modules:
  0.0 57.8 jit_solution(6247090025613151817)
XLA Ops:
  0.6 1.0 %shard_map.153 = (bf16[128,128]{1,0:T(8,128)(2,1)S(1)}, bf16[128,128]{1,0:T(8,128)(2,1)S(1)}, f32[1024,128]{1,0:T(8,128)S(1)}) custom-call(bf16[64,8,128]{2,1,0:T(8,128)(2,1)} %below.1, bf16[64,8,128]{2,1,0:T(8,128)(2,1)} %hidden.1), custom_call_target="tpu_custom_call" | custom-call | bytes 524288 | tf_op jit(solution)/shard_map/pallas_call | solution.py:43
  1.7 0.5 collective-permute-start
  2.2 3.7 %collective-permute-start.1 = (bf16[128,128]{1,0:T(8,128)(2,1)S(1)}, bf16[128,128]{1,0:T(8,128)(2,1)S(1)}, u32[]{:S(2)}, u32[]{:S(2)}) collective-permute-start(bf16[128,128]{1,0:T(8,128)(2,1)S(1)} %get-tuple-element.43), channel_id=1, source_target_pairs={{0,4},{1,5},{2,6},{3,7},{4,0},{5,1},{6,2},{7,3},{8,16},{9,17},{10,... | collective-permute-start | bytes 98312 | tf_op jit(solution)/shard_map/ppermute | solution.py:120
  5.8 1.5 %shard_map.154 = (bf16[8,128,128]{2,1,0:T(8,128)(2,1)S(1)}, f32[128,128]{1,0:T(8,128)S(1)}, f32[512,128]{1,0:T(8,128)S(1)}, bf16[9,256,128]{2,1,0:T(8,128)(2,1)S...) custom-call(f32[1024,128]{1,0:T(8,128)S(1)} %get-tuple-element.40.wi, ...), custom_call_target="tpu_custom_call" | custom-call | bytes 6000000 | tf_op jit(solution)/shard_map/pallas_call | solution.py:43
  7.4 0.0 collective-permute-done.inner.inner_row
  7.4 0.4 collective-permute-done.1.outer.outer_row
  7.7 0.1 shard_map.155
  7.8 5.2 %collective-permute-start.3 = (bf16[128,128]{1,0:T(8,128)(2,1)S(1)}, bf16[128,128]{1,0:T(8,128)(2,1)S(1)}, u32[]{:S(2)}, u32[]{:S(2)}) collective-permute-start(bf16[128,128]{1,0:T(8,128)(2,1)S(1)} %shard_map.155), channel_id=1, source_target_pairs={{0,7},{1,2},{2,1},{3,4},{4,3},{5,6},{6,5},{7,0},{8,15},{9,10},{10,... | collective-permute-start | bytes 98312 | tf_op jit(solution)/shard_map/ppermute | solution.py:120
  13.0 0.0 collective-permute-start.2
  13.0 1.9 %collective-permute-done.3.outer_column = bf16[128,128]{1,0:T(8,128)(2,1)S(1)} collective-permute-done((bf16[128,128]{1,0:T(8,128)(2,1)S(1)}, bf16[128,128]{1,0:T(8,128)(2,1)S(1)}, u32[]{:S(2)}, u32[]{:S(2)}) %collective-permute-start.3) | collective-permute-done | bytes 32800 | tf_op jit(solution)/shard_map/ppermute | solution.py:120
  14.9 2.0 %collective-permute-done.2.inner_column = bf16[128,128]{1,0:T(8,128)(2,1)S(1)} collective-permute-done((bf16[128,128]{1,0:T(8,128)(2,1)S(1)}, bf16[128,128]{1,0:T(8,128)(2,1)S(1)}, u32[]{:S(2)}, u32[]{:S(2)}) %collective-permute-start.2) | collective-permute-done | bytes 32800 | tf_op jit(solution)/shard_map/ppermute | solution.py:120
  16.9 2.5 %shard_map.156 = (bf16[64,8,128]{2,1,0:T(8,128)(2,1)}, f32[512,128]{1,0:T(8,128)}, f32[512,128]{1,0:T(8,128)}, bf16[256,1024]{1,0:T(8,128)(2,1)S(1)}, bf16[256,1...) custom-call(bf16[8,128,128]{2,1,0:T(8,128)(2,1)S(1)} %get-tuple-elem, ...), custom_call_target="tpu_custom_call" | custom-call | flops 1207959552 | bytes 4000000 | tf_op jit(solution)/shard_map/pallas_call | solution.py:43
  19.5 0.1 collective-permute-start.8
  19.5 1.6 %collective-permute-done.8.received = bf16[1168,128]{1,0:T(8,128)(2,1)S(1)} collective-permute-done((bf16[1168,128]{1,0:T(8,128)(2,1)S(1)}, bf16[1168,128]{1,0:T(8,128)(2,1)S(1)}, u32[]{:S(2)}, u32[]{:S(2)}) %collective-permute-start.8) | collective-permute-done | bytes 299040 | tf_op jit(solution)/shard_map/ppermute | solution.py:120
  21.1 0.1 shard_map.159
  21.2 0.1 collective-permute-start.9
  21.3 0.2 collective-permute-start.4
  21.5 0.7 %collective-permute-start.5 = (bf16[256,128]{1,0:T(8,128)(2,1)S(1)}, bf16[256,128]{1,0:T(8,128)(2,1)S(1)}, u32[]{:S(2)}, u32[]{:S(2)}) collective-permute-start(bf16[256,128]{1,0:T(8,128)(2,1)S(1)} %get-tuple-element.57), channel_id=1, source_target_pairs={{0,4},{1,5},{2,6},{3,7},{4,0},{5,1},{6,2},{7,3},{8,16},{9,17},{10,... | collective-permute-start | bytes 196616 | tf_op jit(solution)/shard_map/ppermute | solution.py:120
  22.2 0.4 collective-permute-done.4.inner.inner_row
  22.6 4.7 %collective-permute-done.5.outer.outer_row = bf16[256,128]{1,0:T(8,128)(2,1)S(1)} collective-permute-done((bf16[256,128]{1,0:T(8,128)(2,1)S(1)}, bf16[256,128]{1,0:T(8,128)(2,1)S(1)}, u32[]{:S(2)}, u32[]{:S(2)}) %collective-permute-start.5) | collective-permute-done | bytes 65568 | tf_op jit(solution)/shard_map/ppermute | solution.py:120
  27.4 0.4 shard_map.157.after
  27.8 0.0 collective-permute-done.9.received
  27.8 0.1 shard_map.160
  27.9 1.0 %collective-permute-start.10 = (bf16[304,128]{1,0:T(8,128)(2,1)S(1)}, bf16[304,128]{1,0:T(8,128)(2,1)S(1)}, u32[]{:S(2)}, u32[]{:S(2)}) collective-permute-start(bf16[304,128]{1,0:T(8,128)(2,1)S(1)} %get-tuple-element.69), channel_id=1, source_target_pairs={{0,1},{1,0},{2,3},{3,2},{4,5},{5,4},{6,7},{7,6},{8,24},{9,25},{10,... | collective-permute-start | bytes 233480 | tf_op jit(solution)/shard_map/ppermute | solution.py:120
  28.9 2.7 %collective-permute-start.7 = (bf16[256,128]{1,0:T(8,128)(2,1)S(1)}, bf16[256,128]{1,0:T(8,128)(2,1)S(1)}, u32[]{:S(2)}, u32[]{:S(2)}) collective-permute-start(bf16[256,128]{1,0:T(8,128)(2,1)S(1)} %shard_map.157.after), channel_id=1, source_target_pairs={{0,7},{1,2},{2,1},{3,4},{4,3},{5,6},{6,5},{7,0},{8,15},{9,10},{10,... | collective-permute-start | bytes 196616 | tf_op jit(solution)/shard_map/ppermute | solution.py:120
  31.6 0.0 collective-permute-start.6
  31.6 0.7 %collective-permute-done.10.received = bf16[304,128]{1,0:T(8,128)(2,1)S(1)} collective-permute-done((bf16[304,128]{1,0:T(8,128)(2,1)S(1)}, bf16[304,128]{1,0:T(8,128)(2,1)S(1)}, u32[]{:S(2)}, u32[]{:S(2)}) %collective-permute-start.10) | collective-permute-done | bytes 77856 | tf_op jit(solution)/shard_map/ppermute | solution.py:120
  32.3 0.4 collective-permute-start.11
  32.7 3.6 %collective-permute-done.7.outer_column = bf16[256,128]{1,0:T(8,128)(2,1)S(1)} collective-permute-done((bf16[256,128]{1,0:T(8,128)(2,1)S(1)}, bf16[256,128]{1,0:T(8,128)(2,1)S(1)}, u32[]{:S(2)}, u32[]{:S(2)}) %collective-permute-start.7) | collective-permute-done | bytes 65568 | tf_op jit(solution)/shard_map/ppermute | solution.py:120
  36.4 0.2 collective-permute-done.6.inner_column
  36.6 2.1 %shard_map.158 = (bf16[64,8,128]{2,1,0:T(8,128)(2,1)}, bf16[64,8,128]{2,1,0:T(8,128)(2,1)}, f32[8,128]{1,0:T(8,128)S(1)}) custom-call(bf16[256,1024]{1,0:T(8,128)(2,1)S(1)} %get-tuple-element.55.pre, bf16[256,128]{1,0:T(8,128)(2,1)S(1)} %collective-permute-done.4.inner.inner_row, bf16[256,128]{1,0:T(8,128)(2,1)S(1)} %collective-permute-done.5.outer.outer_row, ...), custom_call_target="tpu_custom_call" | custom-call | flops 603979776 | bytes 2000000 | tf_op jit(solution)/shard_map/pallas_call | solution.py:43
  38.7 0.0 collective-permute-done.11.received
  38.7 0.2 collective-permute-start.12
  38.9 5.1 %collective-permute-done.12.received = bf16[304,128]{1,0:T(8,128)(2,1)S(1)} collective-permute-done((bf16[304,128]{1,0:T(8,128)(2,1)S(1)}, bf16[304,128]{1,0:T(8,128)(2,1)S(1)}, u32[]{:S(2)}, u32[]{:S(2)}) %collective-permute-start.12) | collective-permute-done | bytes 77856 | tf_op jit(solution)/shard_map/ppermute | solution.py:120
  44.1 0.6 collective-permute-start.13
  44.7 4.7 %collective-permute-done.13.received = bf16[304,128]{1,0:T(8,128)(2,1)S(1)} collective-permute-done((bf16[304,128]{1,0:T(8,128)(2,1)S(1)}, bf16[304,128]{1,0:T(8,128)(2,1)S(1)}, u32[]{:S(2)}, u32[]{:S(2)}) %collective-permute-start.13) | collective-permute-done | bytes 77856 | tf_op jit(solution)/shard_map/ppermute | solution.py:120
  49.3 0.1 shard_map.164.own
  49.4 0.1 collective-permute-start.14
  49.5 5.2 %collective-permute-done.14.received = bf16[592,128]{1,0:T(8,128)(2,1)S(1)} collective-permute-done((bf16[592,128]{1,0:T(8,128)(2,1)S(1)}, bf16[592,128]{1,0:T(8,128)(2,1)S(1)}, u32[]{:S(2)}, u32[]{:S(2)}) %collective-permute-start.14) | collective-permute-done | bytes 151584 | tf_op jit(solution)/shard_map/ppermute | solution.py:120
  54.7 0.1 shard_map.165.own
  54.8 0.1 collective-permute-start.15
  54.8 0.9 %shard_map.166.out_before = f32[2304,128]{1,0:T(8,128)} custom-call(bf16[1168,128]{1,0:T(8,128)(2,1)S(1)} %shard_map.165.own), custom_call_target="tpu_custom_call" | custom-call | bytes 884736 | tf_op jit(solution)/shard_map/pallas_call | solution.py:43
  55.7 0.7 %collective-permute-done.15.received = bf16[1168,128]{1,0:T(8,128)(2,1)S(1)} collective-permute-done((bf16[1168,128]{1,0:T(8,128)(2,1)S(1)}, bf16[1168,128]{1,0:T(8,128)(2,1)S(1)}, u32[]{:S(2)}, u32[]{:S(2)}) %collective-permute-start.15) | collective-permute-done | bytes 299040 | tf_op jit(solution)/shard_map/ppermute | solution.py:120
  56.4 1.4 %shard_map.167 = (f32[2304,128]{1,0:T(8,128)}, f32[256]{0:T(256)}) custom-call(bf16[1168,128]{1,0:T(8,128)(2,1)S(1)} %shard_map.165.own, bf16[1168,128]{1,0:T(8,128)(2,1)S(1)} %collective-permute-done.15.received, f32[2304,128]{1,0:T(8,128)} %shard_map.166.out_before), custom_call_target="tpu_custom_call", output_to_operand_aliasing={{0}: (2, {})} | custom-call | bytes 884736 | tf_op jit(solution)/shard_map/pallas_call | solution.py:43
  (3 shorter events, 0.1 us)
Async XLA Ops:
  1.7 5.7 %collective-permute-start = (bf16[128,128]{1,0:T(8,128)(2,1)S(1)}, bf16[128,128]{1,0:T(8,128)(2,1)S(1)}, u32[]{:S(2)}, u32[]{:S(2)}) collective-permute-start(bf16[128,128]{1,0:T(8,128)(2,1)S(1)} %get-tuple-element.42), channel_id=1, source_target_pairs={{0,8},{1,9},{2,10},{3,11},{4,12},{5,13},{6,14},{7,15},{8,0},{9,1},... | collective-permute-start | bytes 98312 | tf_op jit(solution)/shard_map/ppermute | solution.py:120
  2.2 5.6 %collective-permute-start.1 = (bf16[128,128]{1,0:T(8,128)(2,1)S(1)}, bf16[128,128]{1,0:T(8,128)(2,1)S(1)}, u32[]{:S(2)}, u32[]{:S(2)}) collective-permute-start(bf16[128,128]{1,0:T(8,128)(2,1)S(1)} %get-tuple-element.43), channel_id=1, source_target_pairs={{0,4},{1,5},{2,6},{3,7},{4,0},{5,1},{6,2},{7,3},{8,16},{9,17},{10,... | collective-permute-start | bytes 98312 | tf_op jit(solution)/shard_map/ppermute | solution.py:120
  7.8 7.1 %collective-permute-start.3 = (bf16[128,128]{1,0:T(8,128)(2,1)S(1)}, bf16[128,128]{1,0:T(8,128)(2,1)S(1)}, u32[]{:S(2)}, u32[]{:S(2)}) collective-permute-start(bf16[128,128]{1,0:T(8,128)(2,1)S(1)} %shard_map.155), channel_id=1, source_target_pairs={{0,7},{1,2},{2,1},{3,4},{4,3},{5,6},{6,5},{7,0},{8,15},{9,10},{10,... | collective-permute-start | bytes 98312 | tf_op jit(solution)/shard_map/ppermute | solution.py:120
  13.0 3.9 %collective-permute-start.2 = (bf16[128,128]{1,0:T(8,128)(2,1)S(1)}, bf16[128,128]{1,0:T(8,128)(2,1)S(1)}, u32[]{:S(2)}, u32[]{:S(2)}) collective-permute-start(bf16[128,128]{1,0:T(8,128)(2,1)S(1)} %shard_map.155), channel_id=1, source_target_pairs={{0,1},{1,0},{2,3},{3,2},{4,5},{5,4},{6,7},{7,6},{8,9},{9,8},{10,11... | collective-permute-start | bytes 98312 | tf_op jit(solution)/shard_map/ppermute | solution.py:120
  19.5 1.7 %collective-permute-start.8 = (bf16[1168,128]{1,0:T(8,128)(2,1)S(1)}, bf16[1168,128]{1,0:T(8,128)(2,1)S(1)}, u32[]{:S(2)}, u32[]{:S(2)}) collective-permute-start(bf16[1168,128]{1,0:T(8,128)(2,1)S(1)} %get-tuple-element.63), channel_id=1, source_target_pairs={{0,8},{1,9},{2,10},{3,11},{4,12},{5,13},{6,14},{7,15},{8,0},{9,1},... | collective-permute-start | bytes 897032 | tf_op jit(solution)/shard_map/ppermute | solution.py:120
  21.2 6.6 %collective-permute-start.9 = (bf16[592,128]{1,0:T(8,128)(2,1)S(1)}, bf16[592,128]{1,0:T(8,128)(2,1)S(1)}, u32[]{:S(2)}, u32[]{:S(2)}) collective-permute-start(bf16[592,128]{1,0:T(8,128)(2,1)S(1)} %get-tuple-element.66), channel_id=1, source_target_pairs={{0,16},{1,17},{2,18},{3,19},{4,20},{5,21},{6,22},{7,23},{8,9},{9,8... | collective-permute-start | bytes 454664 | tf_op jit(solution)/shard_map/ppermute | solution.py:120
  21.3 1.3 %collective-permute-start.4 = (bf16[256,128]{1,0:T(8,128)(2,1)S(1)}, bf16[256,128]{1,0:T(8,128)(2,1)S(1)}, u32[]{:S(2)}, u32[]{:S(2)}) collective-permute-start(bf16[256,128]{1,0:T(8,128)(2,1)S(1)} %get-tuple-element.56), channel_id=1, source_target_pairs={{0,8},{1,9},{2,10},{3,11},{4,12},{5,13},{6,14},{7,15},{8,0},{9,1},... | collective-permute-start | bytes 196616 | tf_op jit(solution)/shard_map/ppermute | solution.py:120
  21.5 5.8 %collective-permute-start.5 = (bf16[256,128]{1,0:T(8,128)(2,1)S(1)}, bf16[256,128]{1,0:T(8,128)(2,1)S(1)}, u32[]{:S(2)}, u32[]{:S(2)}) collective-permute-start(bf16[256,128]{1,0:T(8,128)(2,1)S(1)} %get-tuple-element.57), channel_id=1, source_target_pairs={{0,4},{1,5},{2,6},{3,7},{4,0},{5,1},{6,2},{7,3},{8,16},{9,17},{10,... | collective-permute-start | bytes 196616 | tf_op jit(solution)/shard_map/ppermute | solution.py:120
  27.9 4.5 %collective-permute-start.10 = (bf16[304,128]{1,0:T(8,128)(2,1)S(1)}, bf16[304,128]{1,0:T(8,128)(2,1)S(1)}, u32[]{:S(2)}, u32[]{:S(2)}) collective-permute-start(bf16[304,128]{1,0:T(8,128)(2,1)S(1)} %get-tuple-element.69), channel_id=1, source_target_pairs={{0,1},{1,0},{2,3},{3,2},{4,5},{5,4},{6,7},{7,6},{8,24},{9,25},{10,... | collective-permute-start | bytes 233480 | tf_op jit(solution)/shard_map/ppermute | solution.py:120
  28.9 7.5 %collective-permute-start.7 = (bf16[256,128]{1,0:T(8,128)(2,1)S(1)}, bf16[256,128]{1,0:T(8,128)(2,1)S(1)}, u32[]{:S(2)}, u32[]{:S(2)}) collective-permute-start(bf16[256,128]{1,0:T(8,128)(2,1)S(1)} %shard_map.157.after), channel_id=1, source_target_pairs={{0,7},{1,2},{2,1},{3,4},{4,3},{5,6},{6,5},{7,0},{8,15},{9,10},{10,... | collective-permute-start | bytes 196616 | tf_op jit(solution)/shard_map/ppermute | solution.py:120
  31.6 5.0 %collective-permute-start.6 = (bf16[256,128]{1,0:T(8,128)(2,1)S(1)}, bf16[256,128]{1,0:T(8,128)(2,1)S(1)}, u32[]{:S(2)}, u32[]{:S(2)}) collective-permute-start(bf16[256,128]{1,0:T(8,128)(2,1)S(1)} %shard_map.157.after), channel_id=1, source_target_pairs={{0,1},{1,0},{2,3},{3,2},{4,5},{5,4},{6,7},{7,6},{8,9},{9,8},{10,11... | collective-permute-start | bytes 196616 | tf_op jit(solution)/shard_map/ppermute | solution.py:120
  32.3 6.3 %collective-permute-start.11 = (bf16[304,128]{1,0:T(8,128)(2,1)S(1)}, bf16[304,128]{1,0:T(8,128)(2,1)S(1)}, u32[]{:S(2)}, u32[]{:S(2)}) collective-permute-start(bf16[304,128]{1,0:T(8,128)(2,1)S(1)} %shard_map.161.own), channel_id=1, source_target_pairs={{0,2},{1,3},{2,0},{3,1},{4,6},{5,7},{6,4},{7,5},{8,12},{9,13},{10,... | collective-permute-start | bytes 233480 | tf_op jit(solution)/shard_map/ppermute | solution.py:120
  38.7 5.4 %collective-permute-start.12 = (bf16[304,128]{1,0:T(8,128)(2,1)S(1)}, bf16[304,128]{1,0:T(8,128)(2,1)S(1)}, u32[]{:S(2)}, u32[]{:S(2)}) collective-permute-start(bf16[304,128]{1,0:T(8,128)(2,1)S(1)} %shard_map.162.own), channel_id=1, source_target_pairs={{0,4},{1,5},{2,6},{3,7},{4,0},{5,1},{6,2},{7,3},{8,10},{9,11},{10,... | collective-permute-start | bytes 233480 | tf_op jit(solution)/shard_map/ppermute | solution.py:120
  44.1 5.3 %collective-permute-start.13 = (bf16[304,128]{1,0:T(8,128)(2,1)S(1)}, bf16[304,128]{1,0:T(8,128)(2,1)S(1)}, u32[]{:S(2)}, u32[]{:S(2)}) collective-permute-start(bf16[304,128]{1,0:T(8,128)(2,1)S(1)} %shard_map.163.own), channel_id=1, source_target_pairs={{0,1},{1,0},{2,3},{3,2},{4,5},{5,4},{6,7},{7,6},{8,24},{9,25},{10,... | collective-permute-start | bytes 233480 | tf_op jit(solution)/shard_map/ppermute | solution.py:120
  49.4 5.3 %collective-permute-start.14 = (bf16[592,128]{1,0:T(8,128)(2,1)S(1)}, bf16[592,128]{1,0:T(8,128)(2,1)S(1)}, u32[]{:S(2)}, u32[]{:S(2)}) collective-permute-start(bf16[592,128]{1,0:T(8,128)(2,1)S(1)} %shard_map.164.own), channel_id=1, source_target_pairs={{0,16},{1,17},{2,18},{3,19},{4,20},{5,21},{6,22},{7,23},{8,9},{9,8... | collective-permute-start | bytes 454664 | tf_op jit(solution)/shard_map/ppermute | solution.py:120
  54.8 1.7 %collective-permute-start.15 = (bf16[1168,128]{1,0:T(8,128)(2,1)S(1)}, bf16[1168,128]{1,0:T(8,128)(2,1)S(1)}, u32[]{:S(2)}, u32[]{:S(2)}) collective-permute-start(bf16[1168,128]{1,0:T(8,128)(2,1)S(1)} %shard_map.165.own), channel_id=1, source_target_pairs={{0,8},{1,9},{2,10},{3,11},{4,12},{5,13},{6,14},{7,15},{8,0},{9,1},... | collective-permute-start | bytes 897032 | tf_op jit(solution)/shard_map/ppermute | solution.py:120
